TPU v7x, 512 devices: a whole 4x8x8 slice. The times are simulated.
512 devices in a mesh: row: 32 (over y, z_lo, core), col: 16 (over x, z_hi).
Axes of the slice: x: 4, y: 8, z: 8 (z_hi: 4, z_lo: 2; z = z_hi * 2 + z_lo), core: 2. Of those that a mesh axis runs over, the one named last changes fastest.
Arguments:
- inputs: bfloat16 [256, 12288], P('col', 'row'), may hold values from -6 to 6
- w_in: bfloat16 [12288, 24576], P('row', 'col'), may hold values from -0.0546875 to 0.0546875
- w_out: bfloat16 [24576, 12288], P('col', 'row'), may hold values from -0.0390625 to 0.0390625
- out_grad: bfloat16 [256, 12288], P('col', 'row'), may hold values from -1.5 to 1.5
Outputs:
- output: bfloat16 [256, 12288], P('col', 'row')
- grad_in: bfloat16 [256, 12288], P('col', 'row')
- grad_w_in: bfloat16 [12288, 24576], P('row', 'col')
- grad_w_out: bfloat16 [24576, 12288], P('col', 'row')
All inputs are finite; a program needn't handle non-finite values.
Results may differ from a plain program's by a relative error of at most 0.005.
Values may be sent and summed in bfloat16 or wider, within the bound.
A program may use at most 64 MiB of HBM per device.

v0:
```python
import jax
import jax.numpy as jnp
from jax import lax
from jax.sharding import PartitionSpec as P

gelu_coef = 0.7978845608028654


def gelu_tanh(value):
    inner = gelu_coef * (value + 0.044715 * value * value * value)
    return 0.5 * value * (1.0 + jnp.tanh(inner))


def gelu_slope(value):
    inner = gelu_coef * (value + 0.044715 * value * value * value)
    tanh_val = jnp.tanh(inner)
    return 0.5 * (1.0 + tanh_val) + 0.5 * value * (1.0 - tanh_val * tanh_val) * gelu_coef * (
        1.0 + 3.0 * 0.044715 * value * value
    )


def on_device(inputs, w_in, w_out, out_grad):
    inputs_all, cotan_all = (
        lax.all_gather(inputs, "col", axis=0, tiled=True),
        lax.all_gather(out_grad, "col", axis=0, tiled=True),
    )
    piece = inputs_all
    pre_share = lax.psum_scatter(
        jnp.dot(piece, w_in, preferred_element_type=jnp.float32),
        "row",
        scatter_dimension=0,
        tiled=True,
    )
    hidden_share = gelu_tanh(pre_share).astype(jnp.bfloat16)
    hidden_all = lax.all_gather(hidden_share, "row", axis=0, tiled=True)
    piece = hidden_all
    output = lax.psum_scatter(
        jnp.dot(piece, w_out, preferred_element_type=jnp.float32),
        "col",
        scatter_dimension=0,
        tiled=True,
    ).astype(jnp.bfloat16)
    piece = cotan_all
    back_share = lax.psum_scatter(
        lax.dot_general(piece, w_out, (((1,), (1,)), ((), ())), preferred_element_type=jnp.float32),
        "row",
        scatter_dimension=0,
        tiled=True,
    )
    grad_share = (back_share * gelu_slope(pre_share)).astype(jnp.bfloat16)
    grad_all = lax.all_gather(grad_share, "row", axis=0, tiled=True)
    grad_w_out = lax.dot_general(
        hidden_all, cotan_all, (((0,), (0,)), ((), ())), preferred_element_type=jnp.float32
    ).astype(jnp.bfloat16)
    grad_w_in = lax.dot_general(
        inputs_all, grad_all, (((0,), (0,)), ((), ())), preferred_element_type=jnp.float32
    ).astype(jnp.bfloat16)
    piece = grad_all
    grad_in = lax.psum_scatter(
        lax.dot_general(piece, w_in, (((1,), (1,)), ((), ())), preferred_element_type=jnp.float32),
        "col",
        scatter_dimension=0,
        tiled=True,
    ).astype(jnp.bfloat16)
    return (output, grad_in, grad_w_in, grad_w_out)


def solution(mesh):
    return jax.shard_map(
        on_device,
        mesh=mesh,
        in_specs=(P("col", "row"), P("row", "col"), P("col", "row"), P("col", "row")),
        out_specs=(P("col", "row"), P("col", "row"), P("row", "col"), P("col", "row")),
        check_vma=False,
    )
```

profile of v0, /device:TPU:1, one launch (start us, length us, event | category | flops | bytes accessed | tf_op | source)
XLA Modules:
  0.0 522.6 jit_solution(16046724008846886201)
XLA Ops:
  7.2 0.0 reduce-scatter.9.cloned.1.call-start
  7.2 44.5 %all_gather.14 = bf16[256,384]{1,0:T(8,128)(2,1)S(1)} all-gather(bf16[16,384]{1,0:T(8,128)(2,1)} %param.7), channel_id=1, replica_groups=mesh['row'=32,'col'=16] {'col'}, dimensions={0}, use_global_device_ids=true | all-gather | bytes 208896 | tf_op jit(solution)/shard_map/all_gather | solution.py:25
  51.7 3.0 fusion.10
  54.7 0.0 reduce-scatter.9.cloned.1.call-update
  54.8 0.0 reduce-scatter.5.cloned.1.call-start
  54.8 0.6 copy-done.1
  55.5 32.7 %all_gather.12 = bf16[256,384]{1,0:T(8,128)(2,1)S(1)} all-gather(bf16[16,384]{1,0:T(8,128)(2,1)S(1)} %copy-done.1), channel_id=1, replica_groups=mesh['row'=32,'col'=16] {'col'}, dimensions={0}, use_global_device_ids=true | all-gather | bytes 208896 | tf_op jit(solution)/shard_map/all_gather | solution.py:24
  88.2 1.7 fusion.8
  89.9 0.0 reduce-scatter.11.cloned.1.call-start
  90.0 84.7 %reduce-scatter.9.cloned.1.call-done = f32[8,1536]{1,0:T(8,128)} async-done(((f32[256,1536]{1,0:T(8,128)}), f32[8,1536]{1,0:T(8,128)}) %reduce-scatter.9.cloned.1.call-update) | async-done | bytes 49168 | tf_op jit(solution)/shard_map/reduce_scatter | solution.py:44
  174.7 120.7 %reduce-scatter.5.cloned.1.call-done = f32[8,1536]{1,0:T(8,128)} async-done(((f32[256,1536]{1,0:T(8,128)}), f32[8,1536]{1,0:T(8,128)}) %reduce-scatter.5.cloned.1.call-update) | async-done | bytes 49168 | tf_op jit(solution)/shard_map/reduce_scatter | solution.py:28
  295.4 0.9 fusion.7
  296.3 35.8 %all_gather.15 = bf16[256,1536]{1,0:T(8,128)(2,1)S(1)} all-gather(bf16[8,1536]{1,0:T(8,128)(2,1)S(1)} %get-tuple-element.8), channel_id=1, replica_groups=mesh['row'=32,'col'=16] {'row'}, dimensions={0}, use_global_device_ids=true | all-gather | bytes 811008 | tf_op jit(solution)/shard_map/all_gather | solution.py:51
  332.1 1.3 fusion.11
  333.5 0.0 reduce-scatter.7.cloned.1.call-start
  333.5 34.8 %all_gather.13 = bf16[256,1536]{1,0:T(8,128)(2,1)S(1)} all-gather(bf16[8,1536]{1,0:T(8,128)(2,1)S(1)} %get-tuple-element.9), channel_id=1, replica_groups=mesh['row'=32,'col'=16] {'row'}, dimensions={0}, use_global_device_ids=true | all-gather | bytes 811008 | tf_op jit(solution)/shard_map/all_gather | solution.py:35
  368.3 2.6 fusion.9
  370.9 1.6 fusion
  372.5 2.4 copy.8
  374.9 1.6 convolution_convert_fusion
  376.5 44.8 %reduce-scatter.11.cloned.1.call-done = f32[16,384]{1,0:T(8,128)} async-done(((f32[256,384]{1,0:T(8,128)}), f32[16,384]{1,0:T(8,128)}) %reduce-scatter.11.cloned.1.call-update) | async-done | bytes 24592 | tf_op jit(solution)/shard_map/reduce_scatter | solution.py:59
  421.4 1.3 convert_element_type.24
  422.7 92.1 %reduce-scatter.7.cloned.1.call-done = f32[16,384]{1,0:T(8,128)} async-done(((f32[256,384]{1,0:T(8,128)}), f32[16,384]{1,0:T(8,128)}) %reduce-scatter.7.cloned.1.call-update) | async-done | bytes 24592 | tf_op jit(solution)/shard_map/reduce_scatter | solution.py:37
  514.8 1.3 convert_element_type.22
  (6 shorter events, 0.1 us)
Async XLA Ops:
  7.2 81.0 %copy-start = (bf16[384,1536]{1,0:T(8,128)(2,1)S(1)}, bf16[384,1536]{1,0:T(8,128)(2,1)}, u32[]{:S(2)}) copy-start(bf16[384,1536]{1,0:T(8,128)(2,1)} %param.5) | copy-start | bytes 3538948
  7.2 167.5 %reduce-scatter.9.cloned.1.call-start = ((), (), s32[]{:S(2)}) async-start(), calls=%async_computation.6 | async-start | bytes 1622016 | tf_op jit(solution)/shard_map/reduce_scatter | solution.py:44
  54.7 0.7 copy-start.1
  54.8 240.7 %reduce-scatter.5.cloned.1.call-start = ((), (), s32[]{:S(2)}) async-start(), calls=%async_computation.4 | async-start | bytes 1622016 | tf_op jit(solution)/shard_map/reduce_scatter | solution.py:28
  89.9 331.4 %reduce-scatter.11.cloned.1.call-start = ((), (), s32[]{:S(2)}) async-start(), calls=%async_computation.7 | async-start | bytes 417792 | tf_op jit(solution)/shard_map/reduce_scatter | solution.py:59
  333.5 181.3 %reduce-scatter.7.cloned.1.call-start = ((), (), s32[]{:S(2)}) async-start(), calls=%async_computation.5 | async-start | bytes 417792 | tf_op jit(solution)/shard_map/reduce_scatter | solution.py:37
Sparse Core Ops, SparseCore 0:
  54.9 119.7 reduce-scatter.8
  177.7 117.6 reduce-scatter.4
  333.6 87.7 reduce-scatter.10
  425.8 88.9 reduce-scatter.6
where the time goes:
time: 524 us; the launch traced here: 523 us
  waiting for transfers between devices  342 us (65%)
  blocking collectives  148 us (28%)
  between operations  13.8 us (3%)
  matrix products  11.9 us (2%)
    reduce_scatter x1, waiting for transfers between devices, on_device(): lax.psum_scatter(jnp.dot(piece, w_in, preferred_element_type=jnp.float32)...  121 us
    reduce_scatter x1, waiting for transfers between devices, on_device(): lax.psum_scatter(jnp.dot(piece, w_out, preferred_element_type=jnp.float32...  92.1 us
    reduce_scatter x1, waiting for transfers between devices, on_device(): lax.psum_scatter(lax.dot_general(piece, w_out, (((1,), (1,)), ((), ())),...  84.7 us
    reduce_scatter x1, waiting for transfers between devices, on_device(): lax.psum_scatter(lax.dot_general(piece, w_in, (((1,), (1,)), ((), ())), p...  44.8 us
    all_gather x1, blocking collectives, on_device(): lax.all_gather(out_grad, 'col', axis=0, tiled=True)  44.5 us
    all_gather x1, blocking collectives, on_device(): grad_all = lax.all_gather(grad_share, 'row', axis=0, tiled=True)  35.8 us
    all_gather x1, blocking collectives, on_device(): hidden_all = lax.all_gather(hidden_share, 'row', axis=0, tiled=True)  34.8 us
    all_gather x1, blocking collectives, on_device(): lax.all_gather(inputs, 'col', axis=0, tiled=True)  32.7 us
  transfers between devices with their start and end apart: 4, of which 4 were waited for; matrix products, arithmetic and copies ran while one was open for 2% of the time, Pallas kernels for 0%

commit v1 on v0

v1 whole, which is shorter than its diff:
```python
import jax
import jax.numpy as jnp
from jax import lax
from jax.experimental import pallas as pl
from jax.experimental.pallas import tpu as pltpu
from jax.sharding import PartitionSpec as P

MESH = pl.DeviceIdType.MESH
BF16, F32 = jnp.bfloat16, jnp.float32
NY, NZL, NK, NX, NZH = 8, 2, 2, 4, 4
TOK, FEAT, HID, HALF = 256, 384, 1536, 768
CHUNK = 16
RING8 = (4, 3, 5, 2, 6, 1, 7)
RING4 = (2, 1, 3)

gelu_coef = 0.7978845608028654


def gelu_and_slope(value):
    inner = gelu_coef * (value + 0.044715 * value * value * value)
    tanh_val = jnp.tanh(inner)
    gelu = 0.5 * value * (1.0 + tanh_val)
    slope = 0.5 * (1.0 + tanh_val) + 0.5 * value * (1.0 - tanh_val * tanh_val) * gelu_coef * (
        1.0 + 3.0 * 0.044715 * value * value
    )
    return gelu, slope


def dot_nn(a, b):
    return lax.dot_general(a, b, (((1,), (0,)), ((), ())), preferred_element_type=F32)


def dot_nt(a, b):
    return lax.dot_general(a, b, (((1,), (1,)), ((), ())), preferred_element_type=F32)


def dot_tn(a, b):
    return lax.dot_general(a, b, (((0,), (0,)), ((), ())), preferred_element_type=F32)


def rows(index, size):
    return pl.ds(pl.multiple_of(index * size, size), size)


def kernel(
    inp_hbm, og_hbm, win_hbm, wout_hbm,
    out_ref, gin_ref, gwin_hbm, gwout_hbm,
    win, wout, win_sib, wout_sib, xall, xsib,
    zsend, zrecv, own, ysend, yrecv, slope_ref, act,
    opart, xrecv, oown, osend, orecv, gwin, gwout,
    ssem, rsem, lsem,
):
    r, col = lax.axis_index("row"), lax.axis_index("col")
    y, zl, k = r // 4, (r // 2) % 2, r % 2
    x, zh = col // 4, col % 4

    def dev(dy=0, dzl=0, dk=0, dx=0, dzh=0):
        row = (((y + dy) % NY) * 2 + (zl + dzl) % 2) * 2 + (k + dk) % 2
        return (row, ((x + dx) % NX) * 4 + (zh + dzh) % NZH)

    partners = (
        [dev(dk=1), dev(dzl=1)]
        + [dev(dzh=d) for d in RING4]
        + [dev(dx=d) for d in RING4]
        + [dev(dy=d) for d in RING8]
    )
    count = [0]
    sent = []

    def send(src, dst, to):
        i = count[0]
        count[0] += 1
        copy = pltpu.make_async_remote_copy(
            src_ref=src, dst_ref=dst, send_sem=ssem.at[i], recv_sem=rsem.at[i],
            device_id=to, device_id_type=MESH,
        )
        copy.start()
        sent.append(copy)
        return copy

    mine = rows(col, CHUNK)
    own_in = [
        pltpu.make_async_copy(inp_hbm, xall.at[0, mine], lsem.at[4]),
        pltpu.make_async_copy(og_hbm, xall.at[1, mine], lsem.at[5]),
    ]
    for copy in own_in:
        copy.start()
    local = []
    for h in range(2):
        cols = pl.ds(h * HALF, HALF)
        local.append(pltpu.make_async_copy(win_hbm.at[:, cols], win.at[h], lsem.at[2 * h]))
        local.append(pltpu.make_async_copy(wout_hbm.at[cols, :], wout.at[h], lsem.at[2 * h + 1]))
    for copy in local:
        copy.start()

    barrier = pltpu.get_barrier_semaphore()
    for partner in partners:
        pl.semaphore_signal(barrier, inc=1, device_id=partner, device_id_type=MESH)
    pl.semaphore_wait(barrier, len(partners))

    a1 = [
        [send(ref, xall.at[a, mine], dev(dzh=d)) for d in RING4] for a, ref in enumerate((inp_hbm, og_hbm))
    ]
    other = rows(1 - k, HALF)
    s_win = send(win_hbm.at[:, other], win_sib, dev(dk=1))
    s_wout = send(wout_hbm.at[other, :], wout_sib, dev(dk=1))
    a2, a3 = [], []
    for a in range(2):
        own_in[a].wait()
        for copy in a1[a]:
            copy.wait_recv()
        block = rows(x, 64)
        a2.append([send(xall.at[a, block], xall.at[a, block], dev(dx=d)) for d in RING4])
        a3.append([send(xall.at[a, block], xsib.at[a, block], dev(dk=1))])
    for a in range(2):
        for d, copy in zip(RING4, a2[a]):
            copy.wait_recv()
            block = rows((x - d) % NX, 64)
            a3[a].append(send(xall.at[a, block], xsib.at[a, block], dev(dk=1)))

    for copy in local:
        copy.wait()
    s_win.wait_recv()
    s_wout.wait_recv()

    zcopy = []
    for a in range(2):
        for copy in a3[a]:
            copy.wait_recv()

        def chip_sum(half):
            block = rows(half, 128)
            if a == 0:
                return dot_nn(xall[a, block, :], win[k]) + dot_nn(xsib[a, block, :], win_sib[...])
            return dot_nt(xall[a, block, :], wout[k]) + dot_nt(xsib[a, block, :], wout_sib[...])

        zsend[a] = chip_sum(1 - zl).astype(BF16)
        zcopy.append(send(zsend.at[a], zrecv.at[a], dev(dzl=1)))
        own[a] = chip_sum(zl)

    ycopy = []
    for a in range(2):
        zcopy[a].wait_recv()
        copies = []
        for d in RING8:
            block = rows((y + d) % NY, CHUNK)
            ysend[a, d] = (own[a, block, :] + zrecv[a, block, :].astype(F32)).astype(BF16)
            copies.append(send(ysend.at[a, d], yrecv.at[a, d], dev(dy=d)))
        ycopy.append(copies)
    ccopy = []
    slot = rows(zl * NY + y, CHUNK)
    for a in range(2):
        block = rows(y, CHUNK)
        total = own[a, block, :] + zrecv[a, block, :].astype(F32)
        for d, copy in zip(RING8, ycopy[a]):
            copy.wait_recv()
            total = total + yrecv[a, d].astype(F32)
        if a == 0:
            hidden, slope = gelu_and_slope(total)
            slope_ref[...] = slope
            act[a, k, slot, :] = hidden.astype(BF16)
        else:
            act[a, k, slot, :] = (total * slope_ref[...]).astype(BF16)
        ref = act.at[a, k, slot]
        by_y = [send(ref, ref, dev(dy=d)) for d in RING8]
        by_z = [send(ref, ref, dev(dzl=1))]
        by_k = [send(ref, ref, dev(dk=1))]
        ccopy.append((by_y, by_z, by_k))

    for a in range(2):
        by_y, by_z, by_k = ccopy[a]
        for d, copy in zip(RING8, by_y):
            copy.wait_recv()
            ref = act.at[a, k, rows(zl * NY + (y - d) % NY, CHUNK)]
            by_z.append(send(ref, ref, dev(dzl=1)))
            by_k.append(send(ref, ref, dev(dk=1)))
        for d, copy in zip((0,) + RING8, by_z):
            copy.wait_recv()
            ref = act.at[a, k, rows((1 - zl) * NY + (y - d) % NY, CHUNK)]
            by_k.append(send(ref, ref, dev(dk=1)))

    xcopy = []
    for a in range(2):
        for copy in ccopy[a][2]:
            copy.wait_recv()
        if a == 0:
            total = dot_nn(act[a, 0], wout[0]) + dot_nn(act[a, 1], wout[1])
        else:
            total = dot_nt(act[a, 0], win[0]) + dot_nt(act[a, 1], win[1])
        oown[a] = total
        opart[a] = total.astype(BF16)
        xcopy.append([
            send(opart.at[a, rows((x + d) % NX, 64)], xrecv.at[a, d], dev(dx=d)) for d in RING4
        ])

    stores = []
    for h in range(2):
        gwout[h] = dot_tn(act[0, h], xall[1]).astype(BF16)
        copy = pltpu.make_async_copy(gwout.at[h], gwout_hbm.at[pl.ds(h * HALF, HALF), :], lsem.at[h])
        copy.start()
        stores.append(copy)

    ocopy = []
    for a in range(2):
        for copy in xcopy[a]:
            copy.wait_recv()
        total = oown[a, rows(x, 64), :]
        for d in RING4:
            total = total + xrecv[a, d].astype(F32)
        oown[a, rows(x, 64), :] = total
        osend[a] = total.astype(BF16)
        ocopy.append([
            send(osend.at[a, rows((zh + d) % NZH, CHUNK)], orecv.at[a, d], dev(dzh=d)) for d in RING4
        ])

    for h in range(2):
        gwin[h] = dot_tn(xall[0], act[1, h]).astype(BF16)
        copy = pltpu.make_async_copy(gwin.at[h], gwin_hbm.at[:, pl.ds(h * HALF, HALF)], lsem.at[2 + h])
        copy.start()
        stores.append(copy)

    for a, ref in enumerate((out_ref, gin_ref)):
        for copy in ocopy[a]:
            copy.wait_recv()
        total = oown[a, rows(col, CHUNK), :]
        for d in RING4:
            total = total + orecv[a, d].astype(F32)
        ref[...] = total.astype(BF16)

    for copy in stores:
        copy.wait()
    for copy in sent:
        copy.wait_send()


N_SENDS = 2 + 2 * (3 + 3 + 4 + 1 + 7 + 7 + 8 + 16 + 3 + 3)


def on_device(inputs, w_in, w_out, out_grad):
    vmem = pl.BlockSpec(memory_space=pltpu.VMEM)
    hbm = pl.BlockSpec(memory_space=pl.ANY)
    flops = 6 * 2 * TOK * FEAT * HID
    return pl.pallas_call(
        kernel,
        out_shape=(
            jax.ShapeDtypeStruct((CHUNK, FEAT), BF16),
            jax.ShapeDtypeStruct((CHUNK, FEAT), BF16),
            jax.ShapeDtypeStruct((FEAT, HID), BF16),
            jax.ShapeDtypeStruct((HID, FEAT), BF16),
        ),
        in_specs=[hbm, hbm, hbm, hbm],
        out_specs=(vmem, vmem, hbm, hbm),
        scratch_shapes=[
            pltpu.VMEM((2, FEAT, HALF), BF16),
            pltpu.VMEM((2, HALF, FEAT), BF16),
            pltpu.VMEM((FEAT, HALF), BF16),
            pltpu.VMEM((HALF, FEAT), BF16),
            pltpu.VMEM((2, TOK, FEAT), BF16),
            pltpu.VMEM((2, TOK, FEAT), BF16),
            pltpu.VMEM((2, 128, HALF), BF16),
            pltpu.VMEM((2, 128, HALF), BF16),
            pltpu.VMEM((2, 128, HALF), F32),
            pltpu.VMEM((2, NY, CHUNK, HALF), BF16),
            pltpu.VMEM((2, NY, CHUNK, HALF), BF16),
            pltpu.VMEM((CHUNK, HALF), F32),
            pltpu.VMEM((2, 2, TOK, HALF), BF16),
            pltpu.VMEM((2, TOK, FEAT), BF16),
            pltpu.VMEM((2, NX, 64, FEAT), BF16),
            pltpu.VMEM((2, TOK, FEAT), F32),
            pltpu.VMEM((2, 64, FEAT), BF16),
            pltpu.VMEM((2, NZH, CHUNK, FEAT), BF16),
            pltpu.VMEM((2, FEAT, HALF), BF16),
            pltpu.VMEM((2, HALF, FEAT), BF16),
            pltpu.SemaphoreType.DMA((N_SENDS,)),
            pltpu.SemaphoreType.DMA((N_SENDS,)),
            pltpu.SemaphoreType.DMA((6,)),
        ],
        compiler_params=pltpu.CompilerParams(
            collective_id=0, has_side_effects=True, vmem_limit_bytes=60 * 1024 * 1024
        ),
        cost_estimate=pl.CostEstimate(flops=flops, bytes_accessed=4 * 2 * FEAT * HID, transcendentals=CHUNK * HALF),
        name="mlp_block",
    )(inputs, out_grad, w_in, w_out)


def solution(mesh):
    return jax.shard_map(
        on_device,
        mesh=mesh,
        in_specs=(P("col", "row"), P("row", "col"), P("col", "row"), P("col", "row")),
        out_specs=(P("col", "row"), P("col", "row"), P("row", "col"), P("col", "row")),
        check_vma=False,
    )
```

time: 524 us -> 76.4 us (0.15)
  waiting for transfers between devices: 342 us -> 0 us
  blocking collectives: 148 us -> 0 us
  Pallas kernels: 0 us -> 69.4 us
  between operations: 13.8 us -> 0.64 us
  matrix products: 11.9 us -> 0 us
    reduce_scatter x4 -> x0, waiting for transfers between devices: 342 us -> none  [the longest x1 121 us: on_device(): lax.psum_scatter(jnp.dot(piece, w_in, preferred_element_type=jnp.float32)...]
    all_gather x4 -> x0, blocking collectives: 148 us -> none  [the longest x1 44.5 us: on_device(): lax.all_gather(out_grad, 'col', axis=0, tiled=True)]
    pallas_call x0 -> x1, Pallas kernels: none -> 69.4 us  [on_device(): pl.pallas_call(kernel, out_shape=(jax.ShapeDtypeStruct((CHUNK, FEAT), BF1...]
    dot_general x6 -> x0, matrix products: 11.9 us -> none  [the longest x1 3.04 us: on_device(): lax.dot_general(piece, w_out, (((1,), (1,)), ((), ())), preferred_element...]
  transfers between devices with their start and end apart: 4 -> 0, of which waited for: 4 -> 0; matrix products, arithmetic and copies ran while one was open for 2% -> 0% of each run, Pallas kernels for 0% -> 0%
where the time goes in v1:
time: 76.4 us; the launch traced here: 76.1 us
  Pallas kernels  69.4 us (91%)
  local copies, waits for them, and re-layouts  6.09 us (8%)
    pallas_call x1, Pallas kernels, on_device(): pl.pallas_call(kernel, out_shape=(jax.ShapeDtypeStruct((CHUNK, FEAT), BF1...  69.4 us
    unnamed x6, local copies, waits for them, and re-layouts  6.09 us

profile of v1, /device:TPU:1, one launch (start us, length us, event | category | flops | bytes accessed | tf_op | source)
XLA Modules:
  0.0 76.1 jit_solution(12050953486235743904)
XLA Ops:
  0.6 69.4 %mlp_block.1 = (bf16[16,384]{1,0:T(8,128)(2,1)}, bf16[16,384]{1,0:T(8,128)(2,1)}, bf16[384,1536]{1,0:T(8,128)(2,1)}, bf16[1536,384]{1,0:T(8,128)(2,1)}) custom-call(bf16[16,384]{1,0:T(8,128)(2,1)} %inp_hbm.1, bf16[16,384]{1,0:T(8,128)(2,1)} %og_hbm.1, bf16[384,1536]{1,0:T(8,128)(2,1)} %win_hbm.1, bf16[1536,384]{1,0:T(8,128)(2,1)} %wout_hbm.1), custom_call_target="tpu_custom_call" | custom-call | flops 1811939328 | bytes 4718592 | tf_op jit(solution)/shard_map/mlp_block/pallas_call | solution.py:243
  70.0 1.3 %copy.12 = bf16[16,384]{1,0:T(8,128)(2,1)} copy(bf16[16,384]{1,0:T(8,128)(2,1)} %get-tuple-element.8) | data formatting | bytes 24576
  71.3 1.3 %copy.13 = bf16[16,384]{1,0:T(8,128)(2,1)} copy(bf16[16,384]{1,0:T(8,128)(2,1)} %get-tuple-element.9) | data formatting | bytes 24576
  72.6 0.0 copy-start
  72.6 2.5 %copy.14 = bf16[384,1536]{1,0:T(8,128)(2,1)} copy(bf16[384,1536]{1,0:T(8,128)(2,1)} %get-tuple-element.10) | data formatting | bytes 2359296
  75.1 0.0 copy-done
  75.1 1.0 %copy.15 = bf16[1536,384]{1,0:T(8,128)(2,1)} copy(bf16[1536,384]{1,0:T(8,128)(2,1)S(1)} %copy-done) | data formatting | bytes 2359296
Async XLA Ops:
  72.6 2.5 %copy-start = (bf16[1536,384]{1,0:T(8,128)(2,1)S(1)}, bf16[1536,384]{1,0:T(8,128)(2,1)}, u32[]{:S(2)}) copy-start(bf16[1536,384]{1,0:T(8,128)(2,1)} %get-tuple-element.11) | copy-start | bytes 3538948

commit v2 on v1

v2 whole, which is shorter than its diff:
```python
import jax
import jax.numpy as jnp
from jax import lax
from jax.experimental import pallas as pl
from jax.experimental.pallas import tpu as pltpu
from jax.sharding import PartitionSpec as P

MESH = pl.DeviceIdType.MESH
BF16, F32 = jnp.bfloat16, jnp.float32
NY, NZL, NK, NX, NZH = 8, 2, 2, 4, 4
TOK, FEAT, HID, HALF = 256, 384, 1536, 768
CHUNK = 16
RING8 = (4, 3, 5, 2, 6, 1, 7)
RING4 = (2, 1, 3)

gelu_coef = 0.7978845608028654


def gelu_and_slope(value):
    inner = gelu_coef * (value + 0.044715 * value * value * value)
    tanh_val = jnp.tanh(inner)
    gelu = 0.5 * value * (1.0 + tanh_val)
    slope = 0.5 * (1.0 + tanh_val) + 0.5 * value * (1.0 - tanh_val * tanh_val) * gelu_coef * (
        1.0 + 3.0 * 0.044715 * value * value
    )
    return gelu, slope


def dot_nn(a, b):
    return lax.dot_general(a, b, (((1,), (0,)), ((), ())), preferred_element_type=F32)


def dot_nt(a, b):
    return lax.dot_general(a, b, (((1,), (1,)), ((), ())), preferred_element_type=F32)


def dot_tn(a, b):
    return lax.dot_general(a, b, (((0,), (0,)), ((), ())), preferred_element_type=F32)


def rows(index, size):
    return pl.ds(pl.multiple_of(index * size, size), size)


def kernel(
    inp_hbm, og_hbm, win_hbm, wout_hbm,
    out_ref, gin_ref, gwin_ref, gwout_ref,
    win, wout, win_sib, wout_sib, xall, xsib,
    zsend, zrecv, own, ysend, yrecv, slope_ref, act,
    opart, xrecv, oown, osend, orecv,
    ssem, rsem, lsem,
):
    r, col = lax.axis_index("row"), lax.axis_index("col")
    y, zl, k = r // 4, (r // 2) % 2, r % 2
    x, zh = col // 4, col % 4

    def dev(dy=0, dzl=0, dk=0, dx=0, dzh=0):
        row = (((y + dy) % NY) * 2 + (zl + dzl) % 2) * 2 + (k + dk) % 2
        return (row, ((x + dx) % NX) * 4 + (zh + dzh) % NZH)

    partners = (
        [dev(dk=1), dev(dzl=1)]
        + [dev(dzh=d) for d in RING4]
        + [dev(dx=d) for d in RING4]
        + [dev(dy=d) for d in RING8]
    )
    count = [0]
    sent = []

    def send(src, dst, to):
        i = count[0]
        count[0] += 1
        copy = pltpu.make_async_remote_copy(
            src_ref=src, dst_ref=dst, send_sem=ssem.at[i], recv_sem=rsem.at[i],
            device_id=to, device_id_type=MESH,
        )
        copy.start()
        sent.append(copy)
        return copy

    own_in = [
        pltpu.make_async_copy(inp_hbm, xall.at[0, x, zh], lsem.at[4]),
        pltpu.make_async_copy(og_hbm, xall.at[1, x, zh], lsem.at[5]),
    ]
    for copy in own_in:
        copy.start()
    local = []
    for h in range(2):
        cols = pl.ds(h * HALF, HALF)
        local.append(pltpu.make_async_copy(win_hbm.at[:, cols], win.at[h], lsem.at[2 * h]))
        local.append(pltpu.make_async_copy(wout_hbm.at[cols, :], wout.at[h], lsem.at[2 * h + 1]))
    for copy in local:
        copy.start()

    barrier = pltpu.get_barrier_semaphore()
    for partner in partners:
        pl.semaphore_signal(barrier, inc=1, device_id=partner, device_id_type=MESH)
    pl.semaphore_wait(barrier, len(partners))

    shards = (inp_hbm, og_hbm)
    by_zh = [[send(ref, xall.at[a, x, zh], dev(dzh=d)) for d in RING4] for a, ref in enumerate(shards)]
    by_x = [[[send(ref, xall.at[a, x, zh], dev(dx=d)) for d in RING4]] for a, ref in enumerate(shards)]
    other = rows(1 - k, HALF)
    s_win = send(win_hbm.at[:, other], win_sib, dev(dk=1))
    s_wout = send(wout_hbm.at[other, :], wout_sib, dev(dk=1))
    for i, d in enumerate(RING4):
        for a in range(2):
            by_zh[a][i].wait_recv()
            ref = xall.at[a, x, (zh - d) % NZH]
            by_x[a].append([send(ref, ref, dev(dx=e)) for e in RING4])

    def pass_to_core(a):
        copies = []
        for d, group in zip((0,) + RING4, by_x[a]):
            if d == 0:
                own_in[a].wait()
            for copy in group:
                copy.wait_recv()
            part = (zh - d) % NZH
            copies.append(send(xall.at[a, :, part], xsib.at[a, :, part], dev(dk=1)))
        return copies

    def chip_sum(a, half):
        block = pl.ds(half * (NX // 2), NX // 2)
        mine, theirs = (ref[a, block].reshape(128, FEAT) for ref in (xall, xsib))
        if a == 0:
            return dot_nn(mine, win[k]) + dot_nn(theirs, win_sib[...])
        return dot_nt(mine, wout[k]) + dot_nt(theirs, wout_sib[...])

    def send_over_z(a):
        zsend[a] = chip_sum(a, 1 - zl).astype(BF16)
        copies = []
        for d in RING8 + (0,):
            block = rows((y + d) % NY, CHUNK)
            copies.append(send(zsend.at[a, block], zrecv.at[a, block], dev(dzl=1)))
        return copies

    def send_over_y(a, zcopy):
        copies = []
        for d, copy in zip(RING8, zcopy):
            copy.wait_recv()
            block = rows((y + d) % NY, CHUNK)
            ysend[a, d] = (own[a, block, :] + zrecv[a, block, :].astype(F32)).astype(BF16)
            copies.append(send(ysend.at[a, d], yrecv.at[a, d], dev(dy=d)))
        return copies

    a3 = pass_to_core(0)
    for copy in local:
        copy.wait()
    s_win.wait_recv()
    for copy in a3:
        copy.wait_recv()
    z0 = send_over_z(0)
    a3 = pass_to_core(1)
    own[0] = chip_sum(0, zl)
    s_wout.wait_recv()
    for copy in a3:
        copy.wait_recv()
    z1 = send_over_z(1)
    y0 = send_over_y(0, z0)
    own[1] = chip_sum(1, zl)
    y1 = send_over_y(1, z1)

    def chunk(a, half, d):
        return act.at[a, k, rows(half * NY + (y + d) % NY, CHUNK)]

    def finish_sum(a, zlast, ycopy):
        zlast.wait_recv()
        block = rows(y, CHUNK)
        total = own[a, block, :] + zrecv[a, block, :].astype(F32)
        for d, copy in zip(RING8, ycopy):
            copy.wait_recv()
            total = total + yrecv[a, d].astype(F32)
        slot = rows(zl * NY + y, CHUNK)
        if a == 0:
            hidden, slope = gelu_and_slope(total)
            slope_ref[...] = slope
            act[a, k, slot, :] = hidden.astype(BF16)
        else:
            act[a, k, slot, :] = (total * slope_ref[...]).astype(BF16)
        ref = chunk(a, zl, 0)
        near = [send(ref, ref, dev(dy=d)) for d in (2, -2, 1, -1)]
        return near, [send(ref, ref, dev(dzl=1))]

    def pass_near(a):
        near, over_z = ccopy[a]
        near[0].wait_recv()
        near[1].wait_recv()
        left, right, far = chunk(a, zl, -2), chunk(a, zl, 2), chunk(a, zl, -2 * turn)
        last = [send(far, far, dev(dy=2 * turn)), send(left, left, dev(dy=1)), send(right, right, dev(dy=-1))]
        over_z += [send(ref, ref, dev(dzl=1)) for ref in (left, right)]
        near[2].wait_recv()
        near[3].wait_recv()
        over_z += [send(ref, ref, dev(dzl=1)) for ref in (chunk(a, zl, -1), chunk(a, zl, 1))]
        return last

    def pass_last(a, last):
        for d, copy in zip((4, -3, 3), last):
            copy.wait_recv()
            ref = chunk(a, zl, d)
            ccopy[a][1].append(send(ref, ref, dev(dzl=1)))
        ref = act.at[a, k, rows(zl, 128)]
        return [send(ref, ref, dev(dk=1))]

    def pass_from_z(a, by_k):
        for d, copy in zip((0, -2, 2, -1, 1, 4, -3, 3), ccopy[a][1]):
            copy.wait_recv()
            ref = chunk(a, 1 - zl, d)
            by_k.append(send(ref, ref, dev(dk=1)))

    def send_over_x(a, by_k):
        for copy in by_k:
            copy.wait_recv()
        if a == 0:
            total = dot_nn(act[a, 0], wout[0]) + dot_nn(act[a, 1], wout[1])
        else:
            total = dot_nt(act[a, 0], win[0]) + dot_nt(act[a, 1], win[1])
        total = total.reshape(NX, NZH, CHUNK, FEAT)
        oown[a] = total
        opart[a] = total.astype(BF16)
        return [
            [
                send(opart.at[a, (x + e) % NX, (zh + d) % NZH], xrecv.at[a, d, e], dev(dx=e))
                for e in RING4
            ]
            for d in RING4 + (0,)
        ]

    def sum_over_x(a, d, copies):
        total = oown[a, x, (zh + d) % NZH]
        for e, copy in zip(RING4, copies):
            copy.wait_recv()
            total = total + xrecv[a, d, e].astype(F32)
        return total

    def send_over_zh(a, xcopy):
        copies = []
        for d, group in zip(RING4, xcopy):
            osend[a, d] = sum_over_x(a, d, group)
            copies.append(send(osend.at[a, d], orecv.at[a, d], dev(dzh=d)))
        return copies

    turn = 1 - 2 * (y % 2)
    ccopy = [finish_sum(0, z0[7], y0)]
    ccopy.append(finish_sum(1, z1[7], y1))
    last0 = pass_near(0)
    last1 = pass_near(1)
    k0 = pass_last(0, last0)
    k1 = pass_last(1, last1)
    pass_from_z(0, k0)
    x0 = send_over_x(0, k0)
    pass_from_z(1, k1)
    x1 = send_over_x(1, k1)
    o0 = send_over_zh(0, x0)
    for h in range(2):
        gwout_ref[pl.ds(h * HALF, HALF), :] = dot_tn(act[0, h], xall[1].reshape(TOK, FEAT)).astype(BF16)
    o1 = send_over_zh(1, x1)
    for h in range(2):
        gwin_ref[:, pl.ds(h * HALF, HALF)] = dot_tn(xall[0].reshape(TOK, FEAT), act[1, h]).astype(BF16)
    for a, (ref, xcopy, copies) in enumerate(((out_ref, x0, o0), (gin_ref, x1, o1))):
        total = sum_over_x(a, 0, xcopy[3])
        for d, copy in zip(RING4, copies):
            copy.wait_recv()
            total = total + orecv[a, d]
        ref[...] = total.astype(BF16)

    for copy in sent:
        copy.wait_send()


N_SENDS = 2 + 2 * (3 + 12 + 4 + 8 + 7 + 7 + 8 + 9 + 12 + 3)


def place(*refs):
    parts = []
    n, sem = (len(refs) - 1) // 2, refs[-1]
    for i in range(n):
        parts.append(pltpu.make_async_copy(refs[i], refs[n + i], sem.at[i]))
        parts[-1].start()
    for part in parts:
        part.wait()


def on_device(inputs, w_in, w_out, out_grad):
    shapes = (
        jax.ShapeDtypeStruct((CHUNK, FEAT), BF16),
        jax.ShapeDtypeStruct((CHUNK, FEAT), BF16),
        jax.ShapeDtypeStruct((FEAT, HID), BF16),
        jax.ShapeDtypeStruct((HID, FEAT), BF16),
    )
    vmem = pl.BlockSpec(memory_space=pltpu.VMEM)
    hbm = pl.BlockSpec(memory_space=pl.ANY)
    flops = 6 * 2 * TOK * FEAT * HID
    results = pl.pallas_call(
        kernel,
        out_shape=shapes,
        in_specs=[hbm, hbm, hbm, hbm],
        out_specs=(vmem, vmem, vmem, vmem),
        scratch_shapes=[
            pltpu.VMEM((2, FEAT, HALF), BF16),
            pltpu.VMEM((2, HALF, FEAT), BF16),
            pltpu.VMEM((FEAT, HALF), BF16),
            pltpu.VMEM((HALF, FEAT), BF16),
            pltpu.VMEM((2, NX, NZH, CHUNK, FEAT), BF16),
            pltpu.VMEM((2, NX, NZH, CHUNK, FEAT), BF16),
            pltpu.VMEM((2, 128, HALF), BF16),
            pltpu.VMEM((2, 128, HALF), BF16),
            pltpu.VMEM((2, 128, HALF), F32),
            pltpu.VMEM((2, NY, CHUNK, HALF), BF16),
            pltpu.VMEM((2, NY, CHUNK, HALF), BF16),
            pltpu.VMEM((CHUNK, HALF), F32),
            pltpu.VMEM((2, 2, TOK, HALF), BF16),
            pltpu.VMEM((2, NX, NZH, CHUNK, FEAT), BF16),
            pltpu.VMEM((2, NZH, NX, CHUNK, FEAT), BF16),
            pltpu.VMEM((2, NX, NZH, CHUNK, FEAT), F32),
            pltpu.VMEM((2, NZH, CHUNK, FEAT), F32),
            pltpu.VMEM((2, NZH, CHUNK, FEAT), F32),
            pltpu.SemaphoreType.DMA((N_SENDS,)),
            pltpu.SemaphoreType.DMA((N_SENDS,)),
            pltpu.SemaphoreType.DMA((6,)),
        ],
        compiler_params=pltpu.CompilerParams(
            collective_id=0, has_side_effects=True, vmem_limit_bytes=40 * 1024 * 1024
        ),
        cost_estimate=pl.CostEstimate(flops=flops, bytes_accessed=4 * 2 * FEAT * HID, transcendentals=CHUNK * HALF),
        name="mlp_block",
    )(*(pltpu.with_memory_space_constraint(v, pltpu.HBM) for v in (inputs, out_grad, w_in, w_out)))
    return pl.pallas_call(
        place,
        out_shape=shapes,
        in_specs=[hbm] * 4,
        out_specs=[hbm] * 4,
        scratch_shapes=[pltpu.SemaphoreType.DMA((4,))],
        compiler_params=pltpu.CompilerParams(vmem_limit_bytes=4 * 1024 * 1024),
        name="place_results",
    )(*results)


def solution(mesh):
    return jax.shard_map(
        on_device,
        mesh=mesh,
        in_specs=(P("col", "row"), P("row", "col"), P("col", "row"), P("col", "row")),
        out_specs=(P("col", "row"), P("col", "row"), P("row", "col"), P("col", "row")),
        check_vma=False,
    )
```

time: 76.4 us -> 66.2 us (0.87)
  local copies, waits for them, and re-layouts: 6.09 us -> 0 us
  Pallas kernels: 69.4 us -> 65.4 us
    unnamed x6 -> x0, local copies, waits for them, and re-layouts: 6.09 us -> none
    pallas_call x1 -> x2, Pallas kernels: 69.4 us -> 65.4 us  [the longest x1 64 us: on_device(): pl.pallas_call(kernel, out_shape=shapes, in_specs=[hbm, hbm, hbm, hbm], o...]
where the time goes in v2:
time: 66.2 us; the launch traced here: 66.1 us
  Pallas kernels  65.4 us (99%)
    pallas_call x1, Pallas kernels, on_device(): pl.pallas_call(kernel, out_shape=shapes, in_specs=[hbm, hbm, hbm, hbm], o...  64 us
    pallas_call x1, Pallas kernels, on_device(): pl.pallas_call(place, out_shape=shapes, in_specs=[hbm] * 4, out_specs=[hb...  1.45 us

profile of v2, /device:TPU:1, one launch (start us, length us, event | category | flops | bytes accessed | tf_op | source)
XLA Modules:
  0.0 66.1 jit_solution(15422045340048166225)
XLA Ops:
  0.6 64.0 %mlp_block.1 = (bf16[16,384]{1,0:T(8,128)(2,1)S(1)}, bf16[16,384]{1,0:T(8,128)(2,1)S(1)}, bf16[384,1536]{1,0:T(8,128)(2,1)S(1)}, bf16[1536,384]{1,0:T(8,128)(2,1)S(1)}) custom-call(bf16[16,384]{1,0:T(8,128)(2,1)} %inp_hbm.1, bf16[16,384]{1,0:T(8,128)(2,1)} %og_hbm.1, bf16[384,1536]{1,0:T(8,128)(2,1)} %win_hbm.1, bf16[1536,384]{1,0:T(8,128)(2,1)} %wout_hbm.1), custom_call_target="tpu_custom_call" | custom-call | flops 1811939328 | bytes 4718592 | tf_op jit(solution)/shard_map/mlp_block/pallas_call | solution.py:294
  64.6 1.4 %place_results.1 = (bf16[16,384]{1,0:T(8,128)(2,1)}, bf16[16,384]{1,0:T(8,128)(2,1)}, bf16[384,1536]{1,0:T(8,128)(2,1)}, bf16[1536,384]{1,0:T(8,128)(2,1)}) custom-call(bf16[16,384]{1,0:T(8,128)(2,1)S(1)} %get-tuple-element.8.refs_0_, bf16[16,384]{1,0:T(8,128)(2,1)S(1)} %get-tuple-element.9.refs_1_, bf16[384,1536]{1,0:T(8,128)(2,1)S(1)} %get-tuple-element.10.refs_2_, ...), custom_call_target="tpu_custom_call" | custom-call | tf_op jit(solution)/shard_map/place_results/pallas_call | solution.py:328

commit v3 on v2

--- a/solution.py
+++ b/solution.py
@@ -46,8 +46,8 @@
     inp_hbm, og_hbm, win_hbm, wout_hbm,
     out_ref, gin_ref, gwin_ref, gwout_ref,
     win, wout, win_sib, wout_sib, xall, xsib,
-    zsend, zrecv, own, ysend, yrecv, slope_ref, act,
-    opart, xrecv, oown, osend, orecv,
+    part, zsend, zrecv, own, ysend, yrecv, slope_ref, act,
+    opart, xrecv, oacc, oown, osend, orecv,
     ssem, rsem, lsem,
 ):
     r, col = lax.axis_index("row"), lax.axis_index("col")
@@ -63,6 +63,7 @@
         + [dev(dzh=d) for d in RING4]
         + [dev(dx=d) for d in RING4]
         + [dev(dy=d) for d in RING8]
+        + [dev(dy=d, dzl=1) for d in (1, -1, 2, -2)]
     )
     count = [0]
     sent = []
@@ -98,20 +99,27 @@
     pl.semaphore_wait(barrier, len(partners))
 
     shards = (inp_hbm, og_hbm)
-    by_zh = [[send(ref, xall.at[a, x, zh], dev(dzh=d)) for d in RING4] for a, ref in enumerate(shards)]
-    by_x = [[[send(ref, xall.at[a, x, zh], dev(dx=d)) for d in RING4]] for a, ref in enumerate(shards)]
+
+    def send_shard(a, over):
+        return [send(shards[a], xall.at[a, x, zh], dev(**{over: d})) for d in RING4]
+
+    by_zh = [send_shard(0, "dzh")]
+    by_x = [[send_shard(0, "dx")]]
+    by_zh.append(send_shard(1, "dzh"))
     other = rows(1 - k, HALF)
     s_win = send(win_hbm.at[:, other], win_sib, dev(dk=1))
     s_wout = send(wout_hbm.at[other, :], wout_sib, dev(dk=1))
-    for i, d in enumerate(RING4):
-        for a in range(2):
-            by_zh[a][i].wait_recv()
+    for a in range(2):
+        if a == 1:
+            by_x.append([send_shard(1, "dx")])
+        for d in (1, 3, 2):
+            by_zh[a][RING4.index(d)].wait_recv()
             ref = xall.at[a, x, (zh - d) % NZH]
             by_x[a].append([send(ref, ref, dev(dx=e)) for e in RING4])
 
     def pass_to_core(a):
         copies = []
-        for d, group in zip((0,) + RING4, by_x[a]):
+        for d, group in zip((0, 1, 3, 2), by_x[a]):
             if d == 0:
                 own_in[a].wait()
             for copy in group:
@@ -120,12 +128,14 @@
             copies.append(send(xall.at[a, :, part], xsib.at[a, :, part], dev(dk=1)))
         return copies
 
+    def own_features(a):
+        mine = xall[a].reshape(TOK, FEAT)
+        part[a] = dot_nn(mine, win[k]) if a == 0 else dot_nt(mine, wout[k])
+
     def chip_sum(a, half):
-        block = pl.ds(half * (NX // 2), NX // 2)
-        mine, theirs = (ref[a, block].reshape(128, FEAT) for ref in (xall, xsib))
-        if a == 0:
-            return dot_nn(mine, win[k]) + dot_nn(theirs, win_sib[...])
-        return dot_nt(mine, wout[k]) + dot_nt(theirs, wout_sib[...])
+        theirs = xsib[a, pl.ds(half * (NX // 2), NX // 2)].reshape(128, FEAT)
+        more = dot_nn(theirs, win_sib[...]) if a == 0 else dot_nt(theirs, wout_sib[...])
+        return part[a, rows(half, 128), :] + more
 
     def send_over_z(a):
         zsend[a] = chip_sum(a, 1 - zl).astype(BF16)
@@ -147,12 +157,14 @@
     a3 = pass_to_core(0)
     for copy in local:
         copy.wait()
+    own_features(0)
     s_win.wait_recv()
     for copy in a3:
         copy.wait_recv()
     z0 = send_over_z(0)
     a3 = pass_to_core(1)
     own[0] = chip_sum(0, zl)
+    own_features(1)
     s_wout.wait_recv()
     for copy in a3:
         copy.wait_recv()
@@ -179,42 +191,47 @@
         else:
             act[a, k, slot, :] = (total * slope_ref[...]).astype(BF16)
         ref = chunk(a, zl, 0)
-        near = [send(ref, ref, dev(dy=d)) for d in (2, -2, 1, -1)]
-        return near, [send(ref, ref, dev(dzl=1))]
+        near = {d: send(ref, ref, dev(dy=d)) for d in (2, -2, 1, -1)}
+        over_z = {0: send(ref, ref, dev(dzl=1))}
+        return near, over_z, [send(ref, ref, dev(dk=1))]
+
+    def pass_on(a, ref):
+        ccopy[a][2].append(send(ref, ref, dev(dk=1)))
 
     def pass_near(a):
-        near, over_z = ccopy[a]
-        near[0].wait_recv()
-        near[1].wait_recv()
+        near, over_z, _ = ccopy[a]
+        near[2].wait_recv()
+        near[-2].wait_recv()
         left, right, far = chunk(a, zl, -2), chunk(a, zl, 2), chunk(a, zl, -2 * turn)
-        last = [send(far, far, dev(dy=2 * turn)), send(left, left, dev(dy=1)), send(right, right, dev(dy=-1))]
-        over_z += [send(ref, ref, dev(dzl=1)) for ref in (left, right)]
-        near[2].wait_recv()
-        near[3].wait_recv()
-        over_z += [send(ref, ref, dev(dzl=1)) for ref in (chunk(a, zl, -1), chunk(a, zl, 1))]
+        last = []
+        for ref, d in ((far, 2 * turn), (left, 1), (right, -1)):
+            last.append([send(ref, ref, dev(dy=d, dzl=dzl)) for dzl in (1, 0)])
+        for d in (-2, 2, -1, 1):
+            if abs(d) == 1:
+                near[-d].wait_recv()
+            ref = chunk(a, zl, d)
+            over_z[d] = send(ref, ref, dev(dzl=1))
+            pass_on(a, ref)
         return last
 
     def pass_last(a, last):
-        for d, copy in zip((4, -3, 3), last):
-            copy.wait_recv()
-            ref = chunk(a, zl, d)
-            ccopy[a][1].append(send(ref, ref, dev(dzl=1)))
-        ref = act.at[a, k, rows(zl, 128)]
-        return [send(ref, ref, dev(dk=1))]
-
-    def pass_from_z(a, by_k):
-        for d, copy in zip((0, -2, 2, -1, 1, 4, -3, 3), ccopy[a][1]):
-            copy.wait_recv()
-            ref = chunk(a, 1 - zl, d)
-            by_k.append(send(ref, ref, dev(dk=1)))
-
-    def send_over_x(a, by_k):
-        for copy in by_k:
-            copy.wait_recv()
-        if a == 0:
-            total = dot_nn(act[a, 0], wout[0]) + dot_nn(act[a, 1], wout[1])
-        else:
-            total = dot_nt(act[a, 0], win[0]) + dot_nt(act[a, 1], win[1])
+        for d in (0, -2, 2, -1, 1):
+            ccopy[a][1][d].wait_recv()
+            pass_on(a, chunk(a, 1 - zl, d))
+        for d, (other_z, same_z) in zip((4, -3, 3), last):
+            same_z.wait_recv()
+            pass_on(a, chunk(a, zl, d))
+            other_z.wait_recv()
+            pass_on(a, chunk(a, 1 - zl, d))
+
+    def model_width(a, half):
+        return dot_nn(act[a, half], wout[half]) if a == 0 else dot_nt(act[a, half], win[half])
+
+    def send_over_x(a):
+        oacc[...] = model_width(a, k)
+        for copy in ccopy[a][2]:
+            copy.wait_recv()
+        total = oacc[...] + model_width(a, 1 - k)
         total = total.reshape(NX, NZH, CHUNK, FEAT)
         oown[a] = total
         opart[a] = total.astype(BF16)
@@ -245,12 +262,10 @@
     ccopy.append(finish_sum(1, z1[7], y1))
     last0 = pass_near(0)
     last1 = pass_near(1)
-    k0 = pass_last(0, last0)
-    k1 = pass_last(1, last1)
-    pass_from_z(0, k0)
-    x0 = send_over_x(0, k0)
-    pass_from_z(1, k1)
-    x1 = send_over_x(1, k1)
+    pass_last(0, last0)
+    x0 = send_over_x(0)
+    pass_last(1, last1)
+    x1 = send_over_x(1)
     o0 = send_over_zh(0, x0)
     for h in range(2):
         gwout_ref[pl.ds(h * HALF, HALF), :] = dot_tn(act[0, h], xall[1].reshape(TOK, FEAT)).astype(BF16)
@@ -268,7 +283,7 @@
         copy.wait_send()
 
 
-N_SENDS = 2 + 2 * (3 + 12 + 4 + 8 + 7 + 7 + 8 + 9 + 12 + 3)
+N_SENDS = 2 + 2 * (3 + 12 + 4 + 8 + 7 + 4 + 6 + 5 + 16 + 12 + 3)
 
 
 def place(*refs):
@@ -303,6 +318,7 @@
             pltpu.VMEM((HALF, FEAT), BF16),
             pltpu.VMEM((2, NX, NZH, CHUNK, FEAT), BF16),
             pltpu.VMEM((2, NX, NZH, CHUNK, FEAT), BF16),
+            pltpu.VMEM((2, TOK, HALF), F32),
             pltpu.VMEM((2, 128, HALF), BF16),
             pltpu.VMEM((2, 128, HALF), BF16),
             pltpu.VMEM((2, 128, HALF), F32),
@@ -312,6 +328,7 @@
             pltpu.VMEM((2, 2, TOK, HALF), BF16),
             pltpu.VMEM((2, NX, NZH, CHUNK, FEAT), BF16),
             pltpu.VMEM((2, NZH, NX, CHUNK, FEAT), BF16),
+            pltpu.VMEM((TOK, FEAT), F32),
             pltpu.VMEM((2, NX, NZH, CHUNK, FEAT), F32),
             pltpu.VMEM((2, NZH, CHUNK, FEAT), F32),
             pltpu.VMEM((2, NZH, CHUNK, FEAT), F32),

time: 66.2 us -> 64.2 us (0.970)
  Pallas kernels: 65.4 us -> 63.2 us
    pallas_call x1, Pallas kernels: 64 us -> 61.7 us  [on_device(): pl.pallas_call(kernel, out_shape=shapes, in_specs=[hbm, hbm, hbm, hbm], o...]
where the time goes in v3:
time: 64.2 us; the launch traced here: 63.8 us
  Pallas kernels  63.2 us (98%)
    pallas_call x1, Pallas kernels, on_device(): pl.pallas_call(kernel, out_shape=shapes, in_specs=[hbm, hbm, hbm, hbm], o...  61.7 us
    pallas_call x1, Pallas kernels, on_device(): pl.pallas_call(place, out_shape=shapes, in_specs=[hbm] * 4, out_specs=[hb...  1.45 us

profile of v3, /device:TPU:1, one launch (start us, length us, event | category | flops | bytes accessed | tf_op | source)
XLA Modules:
  0.0 63.8 jit_solution(8412825818677828739)
XLA Ops:
  0.6 61.7 %mlp_block.1 = (bf16[16,384]{1,0:T(8,128)(2,1)S(1)}, bf16[16,384]{1,0:T(8,128)(2,1)S(1)}, bf16[384,1536]{1,0:T(8,128)(2,1)S(1)}, bf16[1536,384]{1,0:T(8,128)(2,1)S(1)}) custom-call(bf16[16,384]{1,0:T(8,128)(2,1)} %inp_hbm.1, bf16[16,384]{1,0:T(8,128)(2,1)} %og_hbm.1, bf16[384,1536]{1,0:T(8,128)(2,1)} %win_hbm.1, bf16[1536,384]{1,0:T(8,128)(2,1)} %wout_hbm.1), custom_call_target="tpu_custom_call" | custom-call | flops 1811939328 | bytes 4718592 | tf_op jit(solution)/shard_map/mlp_block/pallas_call | solution.py:309
  62.3 1.4 %place_results.1 = (bf16[16,384]{1,0:T(8,128)(2,1)}, bf16[16,384]{1,0:T(8,128)(2,1)}, bf16[384,1536]{1,0:T(8,128)(2,1)}, bf16[1536,384]{1,0:T(8,128)(2,1)}) custom-call(bf16[16,384]{1,0:T(8,128)(2,1)S(1)} %get-tuple-element.8.refs_0_, bf16[16,384]{1,0:T(8,128)(2,1)S(1)} %get-tuple-element.9.refs_1_, bf16[384,1536]{1,0:T(8,128)(2,1)S(1)} %get-tuple-element.10.refs_2_, ...), custom_call_target="tpu_custom_call" | custom-call | tf_op jit(solution)/shard_map/place_results/pallas_call | solution.py:345

commit v4 on v3

--- a/solution.py
+++ b/solution.py
@@ -59,12 +59,18 @@
         return (row, ((x + dx) % NX) * 4 + (zh + dzh) % NZH)
 
     partners = (
-        [dev(dk=1), dev(dzl=1)]
-        + [dev(dzh=d) for d in RING4]
+        [dev(dzh=2), dev(dy=4), dev(dy=3), dev(dy=-3)]
+        + [dev(dzh=d) for d in (1, 3)]
+        + [dev(dy=d, dzl=1) for d in (2, -2)]
+        + [dev(dy=d) for d in (2, -2)]
         + [dev(dx=d) for d in RING4]
-        + [dev(dy=d) for d in RING8]
-        + [dev(dy=d, dzl=1) for d in (1, -1, 2, -2)]
+        + [dev(dy=d, dzl=1) for d in (1, -1)]
+        + [dev(dy=d) for d in (1, -1)]
+        + [dev(dzl=1), dev(dk=1)]
     )
+    barrier = pltpu.get_barrier_semaphore()
+    for partner in partners:
+        pl.semaphore_signal(barrier, inc=1, device_id=partner, device_id_type=MESH)
     count = [0]
     sent = []
 
@@ -93,9 +99,6 @@
     for copy in local:
         copy.start()
 
-    barrier = pltpu.get_barrier_semaphore()
-    for partner in partners:
-        pl.semaphore_signal(barrier, inc=1, device_id=partner, device_id_type=MESH)
     pl.semaphore_wait(barrier, len(partners))
 
     shards = (inp_hbm, og_hbm)
@@ -118,15 +121,11 @@
             by_x[a].append([send(ref, ref, dev(dx=e)) for e in RING4])
 
     def pass_to_core(a):
-        copies = []
-        for d, group in zip((0, 1, 3, 2), by_x[a]):
-            if d == 0:
-                own_in[a].wait()
+        own_in[a].wait()
+        for group in by_x[a]:
             for copy in group:
                 copy.wait_recv()
-            part = (zh - d) % NZH
-            copies.append(send(xall.at[a, :, part], xsib.at[a, :, part], dev(dk=1)))
-        return copies
+        return [send(xall.at[a], xsib.at[a], dev(dk=1))]
 
     def own_features(a):
         mine = xall[a].reshape(TOK, FEAT)
@@ -193,10 +192,7 @@
         ref = chunk(a, zl, 0)
         near = {d: send(ref, ref, dev(dy=d)) for d in (2, -2, 1, -1)}
         over_z = {0: send(ref, ref, dev(dzl=1))}
-        return near, over_z, [send(ref, ref, dev(dk=1))]
-
-    def pass_on(a, ref):
-        ccopy[a][2].append(send(ref, ref, dev(dk=1)))
+        return near, over_z, []
 
     def pass_near(a):
         near, over_z, _ = ccopy[a]
@@ -211,18 +207,14 @@
                 near[-d].wait_recv()
             ref = chunk(a, zl, d)
             over_z[d] = send(ref, ref, dev(dzl=1))
-            pass_on(a, ref)
         return last
 
     def pass_last(a, last):
-        for d in (0, -2, 2, -1, 1):
-            ccopy[a][1][d].wait_recv()
-            pass_on(a, chunk(a, 1 - zl, d))
-        for d, (other_z, same_z) in zip((4, -3, 3), last):
-            same_z.wait_recv()
-            pass_on(a, chunk(a, zl, d))
-            other_z.wait_recv()
-            pass_on(a, chunk(a, 1 - zl, d))
+        for half, copies in ((zl, [c[1] for c in last]), (1 - zl, list(ccopy[a][1].values()) + [c[0] for c in last])):
+            for copy in copies:
+                copy.wait_recv()
+            ref = act.at[a, k, rows(half, 128)]
+            ccopy[a][2].append(send(ref, ref, dev(dk=1)))
 
     def model_width(a, half):
         return dot_nn(act[a, half], wout[half]) if a == 0 else dot_nt(act[a, half], win[half])
@@ -272,6 +264,10 @@
     o1 = send_over_zh(1, x1)
     for h in range(2):
         gwin_ref[:, pl.ds(h * HALF, HALF)] = dot_tn(xall[0].reshape(TOK, FEAT), act[1, h]).astype(BF16)
+    late = o0 + o1
+    for copy in sent:
+        if all(copy is not other for other in late):
+            copy.wait_send()
     for a, (ref, xcopy, copies) in enumerate(((out_ref, x0, o0), (gin_ref, x1, o1))):
         total = sum_over_x(a, 0, xcopy[3])
         for d, copy in zip(RING4, copies):
@@ -279,11 +275,11 @@
             total = total + orecv[a, d]
         ref[...] = total.astype(BF16)
 
-    for copy in sent:
+    for copy in late:
         copy.wait_send()
 
 
-N_SENDS = 2 + 2 * (3 + 12 + 4 + 8 + 7 + 4 + 6 + 5 + 16 + 12 + 3)
+N_SENDS = 2 + 2 * (3 + 12 + 1 + 8 + 7 + 4 + 6 + 5 + 2 + 12 + 3)
 
 
 def place(*refs):

time: 64.2 us -> 63.2 us (0.984)
  Pallas kernels: 63.2 us -> 62.4 us
    pallas_call x1, Pallas kernels: 61.7 us -> 61 us  [on_device(): pl.pallas_call(kernel, out_shape=shapes, in_specs=[hbm, hbm, hbm, hbm], o...]
where the time goes in v4:
time: 63.2 us; the launch traced here: 63.1 us
  Pallas kernels  62.4 us (99%)
  between operations  0.64 us (1%)
    pallas_call x1, Pallas kernels, on_device(): pl.pallas_call(kernel, out_shape=shapes, in_specs=[hbm, hbm, hbm, hbm], o...  61 us
    pallas_call x1, Pallas kernels, on_device(): pl.pallas_call(place, out_shape=shapes, in_specs=[hbm] * 4, out_specs=[hb...  1.45 us

profile of v4, /device:TPU:1, one launch (start us, length us, event | category | flops | bytes accessed | tf_op | source)
XLA Modules:
  0.0 63.1 jit_solution(17209281095373523847)
XLA Ops:
  0.6 61.0 %mlp_block.1 = (bf16[16,384]{1,0:T(8,128)(2,1)S(1)}, bf16[16,384]{1,0:T(8,128)(2,1)S(1)}, bf16[384,1536]{1,0:T(8,128)(2,1)S(1)}, bf16[1536,384]{1,0:T(8,128)(2,1)S(1)}) custom-call(bf16[16,384]{1,0:T(8,128)(2,1)} %inp_hbm.1, bf16[16,384]{1,0:T(8,128)(2,1)} %og_hbm.1, bf16[384,1536]{1,0:T(8,128)(2,1)} %win_hbm.1, bf16[1536,384]{1,0:T(8,128)(2,1)} %wout_hbm.1), custom_call_target="tpu_custom_call" | custom-call | flops 1811939328 | bytes 4718592 | tf_op jit(solution)/shard_map/mlp_block/pallas_call | solution.py:305
  61.6 1.4 %place_results.1 = (bf16[16,384]{1,0:T(8,128)(2,1)}, bf16[16,384]{1,0:T(8,128)(2,1)}, bf16[384,1536]{1,0:T(8,128)(2,1)}, bf16[1536,384]{1,0:T(8,128)(2,1)}) custom-call(bf16[16,384]{1,0:T(8,128)(2,1)S(1)} %get-tuple-element.8.refs_0_, bf16[16,384]{1,0:T(8,128)(2,1)S(1)} %get-tuple-element.9.refs_1_, bf16[384,1536]{1,0:T(8,128)(2,1)S(1)} %get-tuple-element.10.refs_2_, ...), custom_call_target="tpu_custom_call" | custom-call | tf_op jit(solution)/shard_map/place_results/pallas_call | solution.py:341

commit v5 on v4

--- a/solution.py
+++ b/solution.py
@@ -106,15 +106,13 @@
     def send_shard(a, over):
         return [send(shards[a], xall.at[a, x, zh], dev(**{over: d})) for d in RING4]
 
-    by_zh = [send_shard(0, "dzh")]
+    by_zh = [send_shard(0, "dzh"), send_shard(1, "dzh")]
     by_x = [[send_shard(0, "dx")]]
-    by_zh.append(send_shard(1, "dzh"))
     other = rows(1 - k, HALF)
+    by_x.append([send_shard(1, "dx")])
     s_win = send(win_hbm.at[:, other], win_sib, dev(dk=1))
     s_wout = send(wout_hbm.at[other, :], wout_sib, dev(dk=1))
     for a in range(2):
-        if a == 1:
-            by_x.append([send_shard(1, "dx")])
         for d in (1, 3, 2):
             by_zh[a][RING4.index(d)].wait_recv()
             ref = xall.at[a, x, (zh - d) % NZH]
@@ -168,8 +166,8 @@
     for copy in a3:
         copy.wait_recv()
     z1 = send_over_z(1)
+    own[1] = chip_sum(1, zl)
     y0 = send_over_y(0, z0)
-    own[1] = chip_sum(1, zl)
     y1 = send_over_y(1, z1)
 
     def chunk(a, half, d):
@@ -245,7 +243,7 @@
     def send_over_zh(a, xcopy):
         copies = []
         for d, group in zip(RING4, xcopy):
-            osend[a, d] = sum_over_x(a, d, group)
+            osend[a, d] = sum_over_x(a, d, group).astype(BF16)
             copies.append(send(osend.at[a, d], orecv.at[a, d], dev(dzh=d)))
         return copies
 
@@ -272,7 +270,7 @@
         total = sum_over_x(a, 0, xcopy[3])
         for d, copy in zip(RING4, copies):
             copy.wait_recv()
-            total = total + orecv[a, d]
+            total = total + orecv[a, d].astype(F32)
         ref[...] = total.astype(BF16)
 
     for copy in late:
@@ -326,8 +324,8 @@
             pltpu.VMEM((2, NZH, NX, CHUNK, FEAT), BF16),
             pltpu.VMEM((TOK, FEAT), F32),
             pltpu.VMEM((2, NX, NZH, CHUNK, FEAT), F32),
-            pltpu.VMEM((2, NZH, CHUNK, FEAT), F32),
-            pltpu.VMEM((2, NZH, CHUNK, FEAT), F32),
+            pltpu.VMEM((2, NZH, CHUNK, FEAT), BF16),
+            pltpu.VMEM((2, NZH, CHUNK, FEAT), BF16),
             pltpu.SemaphoreType.DMA((N_SENDS,)),
             pltpu.SemaphoreType.DMA((N_SENDS,)),
             pltpu.SemaphoreType.DMA((6,)),

time: 63.2 us -> 62.8 us (level)
  no operation moved by 1% of the time
where the time goes in v5:
time: 62.8 us; the launch traced here: 62.5 us
  Pallas kernels  61.8 us (98%)
  between operations  0.64 us (1%)
    pallas_call x1, Pallas kernels, on_device(): pl.pallas_call(kernel, out_shape=shapes, in_specs=[hbm, hbm, hbm, hbm], o...  60.4 us
    pallas_call x1, Pallas kernels, on_device(): pl.pallas_call(place, out_shape=shapes, in_specs=[hbm] * 4, out_specs=[hb...  1.45 us

profile of v5, /device:TPU:1, one launch (start us, length us, event | category | flops | bytes accessed | tf_op | source)
XLA Modules:
  0.0 62.5 jit_solution(3750938478829012175)
XLA Ops:
  0.6 60.4 %mlp_block.1 = (bf16[16,384]{1,0:T(8,128)(2,1)S(1)}, bf16[16,384]{1,0:T(8,128)(2,1)S(1)}, bf16[384,1536]{1,0:T(8,128)(2,1)S(1)}, bf16[1536,384]{1,0:T(8,128)(2,1)S(1)}) custom-call(bf16[16,384]{1,0:T(8,128)(2,1)} %inp_hbm.1, bf16[16,384]{1,0:T(8,128)(2,1)} %og_hbm.1, bf16[384,1536]{1,0:T(8,128)(2,1)} %win_hbm.1, bf16[1536,384]{1,0:T(8,128)(2,1)} %wout_hbm.1), custom_call_target="tpu_custom_call" | custom-call | flops 1811939328 | bytes 4718592 | tf_op jit(solution)/shard_map/mlp_block/pallas_call | solution.py:303
  61.0 1.4 %place_results.1 = (bf16[16,384]{1,0:T(8,128)(2,1)}, bf16[16,384]{1,0:T(8,128)(2,1)}, bf16[384,1536]{1,0:T(8,128)(2,1)}, bf16[1536,384]{1,0:T(8,128)(2,1)}) custom-call(bf16[16,384]{1,0:T(8,128)(2,1)S(1)} %get-tuple-element.8.refs_0_, bf16[16,384]{1,0:T(8,128)(2,1)S(1)} %get-tuple-element.9.refs_1_, bf16[384,1536]{1,0:T(8,128)(2,1)S(1)} %get-tuple-element.10.refs_2_, ...), custom_call_target="tpu_custom_call" | custom-call | tf_op jit(solution)/shard_map/place_results/pallas_call | solution.py:339
